TPU v7x, 512 devices: a whole 4x4x16 slice. The times are simulated.
512 devices in a mesh: row: 16 (over z_lo, core), col: 8 (over z_hi, y), depth: 4 (over x).
Axes of the slice: x: 4, y: 4, z: 16 (z_hi: 2, z_lo: 8; z = z_hi * 8 + z_lo), core: 2. Of those that a mesh axis runs over, the one named last changes fastest.
Arguments:
- amplitudes: bfloat16 [8192, 256], P(('col', 'depth'), 'row'), may hold values from -6 to 6
- integrals: bfloat16 [16384, 256], P(('row', 'col'), 'depth'), may hold values from -0.375 to 0.375
- old_residual: float32 [8192, 16384], P(('col', 'depth'), 'row'), may hold values from -6 to 6
Outputs:
- new_residual: float32 [8192, 16384], P(('col', 'depth'), 'row')
All inputs are finite; a program needn't handle non-finite values.
Results may differ from a plain program's by a relative error of at most 0.0003.
Values may be sent and summed in bfloat16 or wider, within the bound.
No kernel may reach another device: no remote copies, remote signals or barrier semaphores. Data moves between devices by JAX's collectives and lax.ppermute only.
A program may use at most 64 MiB of HBM per device.

v0:
```python
import jax
import jax.numpy as jnp
from jax import lax
from jax.sharding import PartitionSpec as P


def contract(left, right):
    return lax.dot_general(
        left, right, (((1,), (1,)), ((), ())), preferred_element_type=jnp.float32
    )


def per_device(amplitudes, integrals, old_residual):
    columns = lax.all_gather(integrals, "depth", axis=1, tiled=True)
    integral_full = lax.all_gather(columns, "col", axis=0, tiled=True)
    amp_full = lax.all_gather(amplitudes, "row", axis=1, tiled=True)
    summed = contract(amp_full, integral_full)
    return old_residual + summed


def solution(mesh):
    in_specs = (P(("col", "depth"), "row"), P(("row", "col"), "depth"), P(("col", "depth"), "row"))
    out_specs = P(("col", "depth"), "row")
    return jax.shard_map(
        per_device, mesh=mesh, in_specs=in_specs, out_specs=out_specs, check_vma=False
    )
```

profile of v0, /device:TPU:2, one launch (start us, length us, event | category | flops | bytes accessed | tf_op | source)
XLA Modules:
  0.0 118.2 jit_solution(8433965372696144579)
XLA Ops:
  0.0 0.0 copy-start
  0.0 14.9 %all_gather.10 = bf16[128,256]{0,1:T(8,128)(2,1)S(1)} all-gather(bf16[128,64]{0,1:T(8,128)(2,1)} %param.4), channel_id=1, replica_groups=mesh['row'=16,'col'=8,'depth'=4] {'depth'}, dimensions={1}, use_global_device_ids=true | all-gather | bytes 81920 | tf_op jit(solution)/shard_map/all_gather | solution.py:14
  14.9 0.0 copy-done
  14.9 34.0 %all_gather.9 = bf16[256,256]{0,1:T(8,128)(2,1)S(1)} all-gather(bf16[256,16]{0,1:T(8,128)(2,1)S(1)} %copy-done), channel_id=1, replica_groups=mesh['row'=16,'col'=8,'depth'=4] {'row'}, dimensions={1}, use_global_device_ids=true | all-gather | bytes 139264 | tf_op jit(solution)/shard_map/all_gather | solution.py:16
  49.0 66.7 %all_gather.11 = bf16[1024,256]{0,1:T(8,128)(2,1)S(1)} all-gather(bf16[128,256]{0,1:T(8,128)(2,1)S(1)} %all_gather.10), channel_id=1, replica_groups=mesh['row'=16,'col'=8,'depth'=4] {'col'}, dimensions={0}, use_global_device_ids=true | all-gather | bytes 589824 | tf_op jit(solution)/shard_map/all_gather | solution.py:15
  115.6 2.5 %convolution_add_fusion = f32[256,1024]{1,0:T(8,128)} fusion(f32[256,1024]{1,0:T(8,128)} %param.5, bf16[256,256]{0,1:T(8,128)(2,1)S(1)} %all_gather.9, bf16[1024,256]{0,1:T(8,128)(2,1)S(1)} %all_gather.11), kind=kOutput, calls=%fused_computation | convolution fusion | flops 134479872 | bytes 2752512 | tf_op jit(solution)/shard_map/dot_general | solution.py:8
Async XLA Ops:
  0.0 14.9 %copy-start = (bf16[256,16]{0,1:T(8,128)(2,1)S(1)}, bf16[256,16]{0,1:T(8,128)(2,1)}, u32[]{:S(2)}) copy-start(bf16[256,16]{0,1:T(8,128)(2,1)} %param.3) | copy-start | bytes 24580
where the time goes:
time: 118 us
  blocking collectives  116 us (98%)
  matrix products  2.51 us (2%)
    all_gather x1, blocking collectives, per_device(): integral_full = lax.all_gather(columns, 'col', axis=0, tiled=True)  66.7 us
    all_gather x1, blocking collectives, per_device(): amp_full = lax.all_gather(amplitudes, 'row', axis=1, tiled=True)  34 us
    all_gather x1, blocking collectives, per_device(): columns = lax.all_gather(integrals, 'depth', axis=1, tiled=True)  14.9 us
    dot_general x1, matrix products, contract(): lax.dot_general(left, right, (((1,), (1,)), ((), ())), preferred_element_...  2.51 us

commit v1 on v0

v1 whole, which is shorter than its diff:
```python
import jax
import jax.numpy as jnp
from jax import lax
from jax.experimental import pallas as pl
from jax.experimental.pallas import tpu as pltpu
from jax.sharding import Mesh, PartitionSpec as P

Z_LO, CORES, Z_HI, Y, X = 8, 2, 2, 4, 4
ROW = ("z_lo", "core")
COL = ("z_hi", "y")
PLANE = ("y", "x")


def spread(block, axes, count):
    return lax.all_to_all(jnp.broadcast_to(block[None], (count,) + block.shape), axes, 0, 0)


def ladder_kernel(amp_ref, int_ref, old_ref, new_ref, held, sems):
    rows, width = held.shape[1:]
    amp = amp_ref[...].reshape(-1, rows)
    copies = []
    for part in range(held.shape[0]):
        half, pair = divmod(part, Y // 2)
        panels = []
        for y in (2 * pair, 2 * pair + 1):
            panel = int_ref[y * X:(y + 1) * X, half]
            panels.append(panel.reshape(-1, panel.shape[-1]))
        product = lax.dot_general(
            amp,
            jnp.concatenate(panels, axis=1),
            (((0,), (0,)), ((), ())),
            preferred_element_type=jnp.float32,
        )
        columns = pl.ds(part * width, width)
        held[part] = old_ref[:, columns] + product
        copy = pltpu.make_async_copy(held.at[part], new_ref.at[:, columns], sems.at[part])
        copy.start()
        copies.append(copy)
    for copy in copies:
        copy.wait()


def add_ladder(amp, integrals, old):
    parts = Z_HI * Y // 2
    rows, columns = old.shape
    vmem = pl.BlockSpec(memory_space=pltpu.VMEM)
    return pl.pallas_call(
        ladder_kernel,
        out_shape=jax.ShapeDtypeStruct(old.shape, old.dtype),
        in_specs=[vmem, vmem, vmem],
        out_specs=pl.BlockSpec(memory_space=pl.ANY),
        scratch_shapes=[
            pltpu.VMEM((parts, rows, columns // parts), jnp.float32),
            pltpu.SemaphoreType.DMA((parts,)),
        ],
        compiler_params=pltpu.CompilerParams(vmem_limit_bytes=32 * 1024 * 1024),
        cost_estimate=pl.CostEstimate(
            flops=2 * 256 * rows * columns, bytes_accessed=8 * rows * columns, transcendentals=0
        ),
    )(amp, integrals, old)


def per_device(amplitudes, integrals, old_residual):
    mine = integrals.T
    other = lax.ppermute(mine, "z_hi", [(0, 1), (1, 0)])
    amp_full = spread(amplitudes.T, ROW, Z_LO * CORES)
    low = lax.axis_index("z_hi") == 0
    both = jnp.stack([jnp.where(low, mine, other), jnp.where(low, other, mine)])
    integral_full = spread(both, PLANE, Y * X)
    return add_ladder(amp_full, integral_full, old_residual)


def solution(mesh):
    devices = mesh.devices.reshape(Z_LO, CORES, Z_HI, Y, X)
    fine = Mesh(devices, ROW + COL + ("x",))
    in_specs = (P(COL + ("x",), ROW), P(ROW + COL, "x"), P(COL + ("x",), ROW))
    out_specs = P(COL + ("x",), ROW)
    return jax.shard_map(
        per_device, mesh=fine, in_specs=in_specs, out_specs=out_specs, check_vma=False
    )
```

time: 118 us -> 47.9 us (0.41)
  the two profiles are of different devices: /device:TPU:2 before, /device:TPU:32 now
where the time goes in v1:
time: 47.9 us; the launch traced here: 47.6 us
  starting transfers between devices  20.9 us (44%)
  blocking collectives  17.5 us (37%)
  waiting for transfers between devices  6.44 us (13%)
  local copies, waits for them, and re-layouts  1.57 us (3%)
  Pallas kernels  1.26 us (3%)
    all_to_all x1, blocking collectives, spread(): lax.all_to_all(jnp.broadcast_to(block[None], (count,) + block.shape), axe...  17.5 us
    all_to_all x1, starting transfers between devices, spread(): lax.all_to_all(jnp.broadcast_to(block[None], (count,) + block.shape), axe...  12.6 us
    ppermute x1, starting transfers between devices, per_device(): other = lax.ppermute(mine, 'z_hi', [(0, 1), (1, 0)])  8.21 us
    ppermute x1, waiting for transfers between devices, per_device(): other = lax.ppermute(mine, 'z_hi', [(0, 1), (1, 0)])  6.43 us
    broadcast_in_dim x2, local copies, waits for them, and re-layouts, spread(): jnp.broadcast_to(block[None], (count,) + block.shape)  1.56 us
    pallas_call x1, Pallas kernels, add_ladder(): pl.pallas_call(ladder_kernel, out_shape=jax.ShapeDtypeStruct(old.shape, o...  1.26 us
  transfers between devices with their start and end apart: 2, of which 1 were waited for; matrix products, arithmetic and copies ran while one was open for 0% of the time, Pallas kernels for 0%

profile of v1, /device:TPU:32, one launch (start us, length us, event | category | flops | bytes accessed | tf_op | source)
XLA Modules:
  0.0 47.6 jit_solution(1837503624117864309)
XLA Ops:
  0.0 0.0 copy-start.1
  0.0 0.0 copy-start
  0.0 1.4 %broadcast_in_dim.4 = bf16[16,16,256]{2,1,0:T(8,128)(2,1)} broadcast(bf16[16,256]{1,0:T(8,128)(2,1)} %bitcast.9), dimensions={1,2} | broadcast | bytes 139264 | tf_op jit(solution)/shard_map/broadcast_in_dim | solution.py:15
  1.5 12.6 %all-to-all-start = ((bf16[16,16,256]{2,1,0:T(8,128)(2,1)}), bf16[16,16,256]{2,1,0:T(8,128)(2,1)S(1)}, u32[]{:S(2)}, u32[]{:S(2)}) async-start(bf16[16,16,256]{2,1,0:T(8,128)(2,1)} %broadcast_in_dim.4), calls=%async_computation | async-start | bytes 262144 | tf_op jit(solution)/shard_map/all_to_all | solution.py:15
  14.1 8.2 %collective-permute-start = (bf16[64,128]{1,0:T(8,128)(2,1)}, bf16[64,128]{1,0:T(8,128)(2,1)S(1)}, u32[]{:S(2)}, u32[]{:S(2)}) collective-permute-start(bf16[64,128]{1,0:T(8,128)(2,1)} %bitcast.8), channel_id=1, source_target_pairs={{0,16},{16,0},{1,17},{17,1},{2,18},{18,2},{3,19},{19,3},{4,20},{20... | collective-permute-start | bytes 49160 | tf_op jit(solution)/shard_map/ppermute | solution.py:65
  22.3 6.4 %collective-permute-done = bf16[64,128]{1,0:T(8,128)(2,1)S(1)} collective-permute-done((bf16[64,128]{1,0:T(8,128)(2,1)}, bf16[64,128]{1,0:T(8,128)(2,1)S(1)}, u32[]{:S(2)}, u32[]{:S(2)}) %collective-permute-start) | collective-permute-done | bytes 16416 | tf_op jit(solution)/shard_map/ppermute | solution.py:65
  28.8 0.0 copy-done.1
  28.8 0.0 all-to-all-done.amp_ref
  28.8 0.1 broadcast_in_dim.5
  28.9 17.5 %all_to_all.10.int_ref = bf16[16,2,64,128]{3,2,1,0:T(8,128)(2,1)S(1)} all-to-all(bf16[16,2,64,128]{3,2,1,0:T(8,128)(2,1)S(1)} %broadcast_in_dim.5), channel_id=1, replica_groups=mesh['z_lo'=8,'core'=2,'z_hi'=2,'y'=4,'x'=4] {'y','x'}, dimensions={0} | all-to-all | bytes 1048576 | tf_op jit(solution)/shard_map/all_to_all | solution.py:15
  46.4 0.0 copy-done
  46.4 1.3 %shard_map.37 = f32[256,1024]{1,0:T(8,128)} custom-call(bf16[16,16,256]{2,1,0:T(8,128)(2,1)S(1)} %all-to-all-done.amp_ref, bf16[16,2,64,128]{3,2,1,0:T(8,128)(2,1)S(1)} %all_to_all.10.int_ref, f32[256,1024]{1,0:T(8,128)S(1)} %copy-done), custom_call_target="tpu_custom_call" | custom-call | flops 134217728 | bytes 2097152 | tf_op jit(solution)/shard_map/pallas_call | solution.py:47
  (2 shorter events, 0.0 us)
Async XLA Ops:
  0.0 28.8 %copy-start.1 = (bf16[128,64]{0,1:T(8,128)(2,1)S(1)}, bf16[128,64]{0,1:T(8,128)(2,1)}, u32[]{:S(2)}) copy-start(bf16[128,64]{0,1:T(8,128)(2,1)} %param.4) | copy-start | bytes 49156
  0.0 46.4 %copy-start = (f32[256,1024]{1,0:T(8,128)S(1)}, f32[256,1024]{1,0:T(8,128)}, u32[]{:S(2)}) copy-start(f32[256,1024]{1,0:T(8,128)} %old_ref.1) | copy-start | bytes 3145732
  1.5 27.3 %all-to-all-start = ((bf16[16,16,256]{2,1,0:T(8,128)(2,1)}), bf16[16,16,256]{2,1,0:T(8,128)(2,1)S(1)}, u32[]{:S(2)}, u32[]{:S(2)}) async-start(bf16[16,16,256]{2,1,0:T(8,128)(2,1)} %broadcast_in_dim.4), calls=%async_computation | async-start | bytes 262144 | tf_op jit(solution)/shard_map/all_to_all | solution.py:15
  14.1 14.7 %collective-permute-start = (bf16[64,128]{1,0:T(8,128)(2,1)}, bf16[64,128]{1,0:T(8,128)(2,1)S(1)}, u32[]{:S(2)}, u32[]{:S(2)}) collective-permute-start(bf16[64,128]{1,0:T(8,128)(2,1)} %bitcast.8), channel_id=1, source_target_pairs={{0,16},{16,0},{1,17},{17,1},{2,18},{18,2},{3,19},{19,3},{4,20},{20... | collective-permute-start | bytes 49160 | tf_op jit(solution)/shard_map/ppermute | solution.py:65

commit v2 on v1

--- a/solution.py
+++ b/solution.py
@@ -62,10 +62,8 @@
 
 def per_device(amplitudes, integrals, old_residual):
     mine = integrals.T
-    other = lax.ppermute(mine, "z_hi", [(0, 1), (1, 0)])
     amp_full = spread(amplitudes.T, ROW, Z_LO * CORES)
-    low = lax.axis_index("z_hi") == 0
-    both = jnp.stack([jnp.where(low, mine, other), jnp.where(low, other, mine)])
+    both = lax.all_gather(mine, "z_hi")
     integral_full = spread(both, PLANE, Y * X)
     return add_ladder(amp_full, integral_full, old_residual)
 

time: 47.9 us -> 47 us (0.981)
  the two profiles are of different devices: /device:TPU:32 before, /device:TPU:128 now
where the time goes in v2:
time: 47 us; the launch traced here: 46.7 us
  blocking collectives  32.6 us (69%)
  starting transfers between devices  11.3 us (24%)
  local copies, waits for them, and re-layouts  1.56 us (3%)
  Pallas kernels  1.26 us (3%)
    all_to_all x1, blocking collectives, spread(): lax.all_to_all(jnp.broadcast_to(block[None], (count,) + block.shape), axe...  18.6 us
    all_gather x1, blocking collectives, per_device(): both = lax.all_gather(mine, 'z_hi')  14 us
    all_to_all x1, starting transfers between devices, spread(): lax.all_to_all(jnp.broadcast_to(block[None], (count,) + block.shape), axe...  11.3 us
    broadcast_in_dim x2, local copies, waits for them, and re-layouts, spread(): jnp.broadcast_to(block[None], (count,) + block.shape)  1.56 us
    pallas_call x1, Pallas kernels, add_ladder(): pl.pallas_call(ladder_kernel, out_shape=jax.ShapeDtypeStruct(old.shape, o...  1.26 us
  transfers between devices with their start and end apart: 1, of which 0 were waited for; matrix products, arithmetic and copies ran while one was open for 0% of the time, Pallas kernels for 0%

profile of v2, /device:TPU:128, one launch (start us, length us, event | category | flops | bytes accessed | tf_op | source)
XLA Modules:
  0.0 46.7 jit_solution(13341721214182509899)
XLA Ops:
  0.0 0.0 copy-start
  0.0 1.4 %broadcast_in_dim.4 = bf16[16,16,256]{2,1,0:T(8,128)(2,1)} broadcast(bf16[16,256]{1,0:T(8,128)(2,1)} %bitcast.5), dimensions={1,2} | broadcast | bytes 139264 | tf_op jit(solution)/shard_map/broadcast_in_dim | solution.py:15
  1.5 11.3 %all-to-all-start = ((bf16[16,16,256]{2,1,0:T(8,128)(2,1)}), bf16[16,16,256]{2,1,0:T(8,128)(2,1)S(1)}, u32[]{:S(2)}, u32[]{:S(2)}) async-start(bf16[16,16,256]{2,1,0:T(8,128)(2,1)} %broadcast_in_dim.4), calls=%async_computation | async-start | bytes 262144 | tf_op jit(solution)/shard_map/all_to_all | solution.py:15
  12.7 14.0 %all-gather = bf16[128,128]{1,0:T(8,128)(2,1)S(1)} all-gather(bf16[64,128]{1,0:T(8,128)(2,1)} %bitcast.4), channel_id=2, replica_groups=mesh['z_lo'=8,'core'=2,'z_hi'=2,'y'=4,'x'=4] {'z_hi'}, dimensions={0}, use_global_device_ids=true | all-gather | bytes 49152 | tf_op jit(solution)/shard_map/all_gather | solution.py:66
  26.7 0.0 all-to-all-done.amp_ref
  26.7 0.1 broadcast_in_dim.5
  26.8 18.6 %all_to_all.10.int_ref = bf16[16,2,64,128]{3,2,1,0:T(8,128)(2,1)S(1)} all-to-all(bf16[16,2,64,128]{3,2,1,0:T(8,128)(2,1)S(1)} %broadcast_in_dim.5), channel_id=1, replica_groups=mesh['z_lo'=8,'core'=2,'z_hi'=2,'y'=4,'x'=4] {'y','x'}, dimensions={0} | all-to-all | bytes 1048576 | tf_op jit(solution)/shard_map/all_to_all | solution.py:15
  45.4 0.0 copy-done
  45.4 1.3 %shard_map.37 = f32[256,1024]{1,0:T(8,128)} custom-call(bf16[16,16,256]{2,1,0:T(8,128)(2,1)S(1)} %all-to-all-done.amp_ref, bf16[16,2,64,128]{3,2,1,0:T(8,128)(2,1)S(1)} %all_to_all.10.int_ref, f32[256,1024]{1,0:T(8,128)S(1)} %copy-done), custom_call_target="tpu_custom_call" | custom-call | flops 134217728 | bytes 2097152 | tf_op jit(solution)/shard_map/pallas_call | solution.py:47
Async XLA Ops:
  0.0 45.4 %copy-start = (f32[256,1024]{1,0:T(8,128)S(1)}, f32[256,1024]{1,0:T(8,128)}, u32[]{:S(2)}) copy-start(f32[256,1024]{1,0:T(8,128)} %old_ref.1) | copy-start | bytes 3145732
  1.5 25.2 %all-to-all-start = ((bf16[16,16,256]{2,1,0:T(8,128)(2,1)}), bf16[16,16,256]{2,1,0:T(8,128)(2,1)S(1)}, u32[]{:S(2)}, u32[]{:S(2)}) async-start(bf16[16,16,256]{2,1,0:T(8,128)(2,1)} %broadcast_in_dim.4), calls=%async_computation | async-start | bytes 262144 | tf_op jit(solution)/shard_map/all_to_all | solution.py:15

commit v3 on v2

--- a/solution.py
+++ b/solution.py
@@ -9,22 +9,24 @@
 ROW = ("z_lo", "core")
 COL = ("z_hi", "y")
 PLANE = ("y", "x")
+Z_ORDER = (5, 6, 7, 4, 3, 2, 1, 0)
+PLANE_ORDER = tuple((10 + i) % (Y * X) for i in range(Y * X))
 
 
-def spread(block, axes, count):
-    return lax.all_to_all(jnp.broadcast_to(block[None], (count,) + block.shape), axes, 0, 0)
+def spread(block, axes, order):
+    copies = jnp.broadcast_to(block[None], (len(order),) + block.shape)
+    return lax.all_to_all(copies, axes, 0, 0, axis_index_groups=[list(order)])
 
 
 def ladder_kernel(amp_ref, int_ref, old_ref, new_ref, held, sems):
     rows, width = held.shape[1:]
-    amp = amp_ref[...].reshape(-1, rows)
+    amp = jnp.concatenate([amp_ref[Z_ORDER.index(z), c] for z in range(Z_LO) for c in range(CORES)])
     copies = []
     for part in range(held.shape[0]):
         half, pair = divmod(part, Y // 2)
         panels = []
         for y in (2 * pair, 2 * pair + 1):
-            panel = int_ref[y * X:(y + 1) * X, half]
-            panels.append(panel.reshape(-1, panel.shape[-1]))
+            panels.append(jnp.concatenate([int_ref[PLANE_ORDER.index(y * X + x), half] for x in range(X)]))
         product = lax.dot_general(
             amp,
             jnp.concatenate(panels, axis=1),
@@ -61,10 +63,21 @@
 
 
 def per_device(amplitudes, integrals, old_residual):
-    mine = integrals.T
-    amp_full = spread(amplitudes.T, ROW, Z_LO * CORES)
-    both = lax.all_gather(mine, "z_hi")
-    integral_full = spread(both, PLANE, Y * X)
+    low = lax.axis_index("z_hi") == 0
+    mine, amp = integrals.T, amplitudes.T
+    down = lax.ppermute(mine, "z_hi", [(1, 0)])
+    near = lax.cond(
+        low,
+        lambda a: spread(a, "z_lo", Z_ORDER),
+        lambda a: jnp.zeros((Z_LO,) + a.shape, a.dtype),
+        amp,
+    )
+    again, near = lax.optimization_barrier((mine, near))
+    up = lax.ppermute(again, "z_hi", [(0, 1)])
+    near = lax.cond(low, lambda a, n: n, lambda a, n: spread(a, "z_lo", Z_ORDER), amp, near)
+    amp_full = lax.all_gather(near, "core", axis=1)
+    both = jnp.stack([jnp.where(low, mine, up), jnp.where(low, down, mine)])
+    integral_full = spread(both, PLANE, PLANE_ORDER)
     return add_ladder(amp_full, integral_full, old_residual)
 
 

time: 47 us -> 39 us (0.83)
  the two profiles are of different devices: /device:TPU:128 before, /device:TPU:480 now
where the time goes in v3:
time: 39 us; the launch traced here: 38.7 us
  starting transfers between devices  16.9 us (43%)
  blocking collectives  14.5 us (37%)
  waiting for transfers between devices  4.28 us (11%)
  local copies, waits for them, and re-layouts  1.65 us (4%)
  Pallas kernels  1.26 us (3%)
    all_to_all x1, blocking collectives, spread(): return lax.all_to_all(copies, axes, 0, 0, axis_index_groups=[list(order)])  12.6 us
    all_to_all x1, starting transfers between devices, spread(): return lax.all_to_all(copies, axes, 0, 0, axis_index_groups=[list(order)])  9.05 us
    ppermute x1, starting transfers between devices, per_device(): down = lax.ppermute(mine, 'z_hi', [(1, 0)])  6.45 us
    all_to_all x1, waiting for transfers between devices, spread(): return lax.all_to_all(copies, axes, 0, 0, axis_index_groups=[list(order)])  3.27 us
    all_gather x1, blocking collectives, per_device(): amp_full = lax.all_gather(near, 'core', axis=1)  1.89 us
    ppermute x1, starting transfers between devices, per_device(): up = lax.ppermute(again, 'z_hi', [(0, 1)])  1.41 us
    pallas_call x1, Pallas kernels, add_ladder(): pl.pallas_call(ladder_kernel, out_shape=jax.ShapeDtypeStruct(old.shape, o...  1.26 us
    ppermute x1, waiting for transfers between devices, per_device(): up = lax.ppermute(again, 'z_hi', [(0, 1)])  1.01 us
  transfers between devices with their start and end apart: 3, of which 2 were waited for; matrix products, arithmetic and copies ran while one was open for 0% of the time, Pallas kernels for 0%

profile of v3, /device:TPU:480, one launch (start us, length us, event | category | flops | bytes accessed | tf_op | source)
XLA Modules:
  0.0 38.7 jit_solution(15984872469877223579)
XLA Ops:
  0.0 0.0 copy-start.1
  0.0 6.5 %collective-permute-start.1 = (bf16[64,128]{1,0:T(8,128)(2,1)}, bf16[64,128]{1,0:T(8,128)(2,1)S(1)}, u32[]{:S(2)}, u32[]{:S(2)}) collective-permute-start(bf16[64,128]{1,0:T(8,128)(2,1)} %bitcast.12), channel_id=1, source_target_pairs={{16,0},{17,1},{18,2},{19,3},{20,4},{21,5},{22,6},{23,7},{24,8},{25... | collective-permute-start | bytes 49160 | tf_op jit(solution)/shard_map/ppermute | solution.py:68
  6.5 0.0 copy-done.1
  6.5 0.0 copy-start.2
  6.5 0.7 %copy-done.2 = bf16[128,64]{0,1:T(8,128)(2,1)S(1)} copy-done((bf16[128,64]{0,1:T(8,128)(2,1)S(1)}, bf16[128,64]{0,1:T(8,128)(2,1)}, u32[]{:S(2)}) %copy-start.2) | copy-done | bytes 16408
  7.2 0.0 copy-start
  7.2 1.4 %collective-permute-start = (bf16[64,128]{1,0:T(8,128)(2,1)S(1)}, bf16[64,128]{1,0:T(8,128)(2,1)S(1)}, u32[]{:S(2)}, u32[]{:S(2)}) collective-permute-start(bf16[64,128]{1,0:T(8,128)(2,1)S(1)} %bitcast.13), channel_id=1, source_target_pairs={{0,16},{1,17},{2,18},{3,19},{4,20},{5,21},{6,22},{7,23},{8,24},{9,... | collective-permute-start | bytes 49160 | tf_op jit(solution)/shard_map/ppermute | solution.py:76
  8.7 12.6 %conditional.3 = (bf16[8,16,256]{2,1,0:T(8,128)(2,1)S(1)}) conditional(s32[]{:T(128)} %convert_element_type.4, bf16[16,256]{1,0:T(8,128)(2,1)S(1)} %bitcast.11, bf16[8,16,256]{2,1,0:T(8,128)(2,1)S(1)} %get-tuple-element.20), branch_computations={%region_2.0_spmd, %region_3.0_spmd} | conditional | bytes 204808 | solution.py:77
  8.7 12.6 %all_to_all.14 = bf16[8,16,256]{2,1,0:T(8,128)(2,1)S(1)} all-to-all(bf16[8,16,256]{2,1,0:T(8,128)(2,1)S(1)} %broadcast_in_dim.8), channel_id=1, replica_groups={{320,384,448,256,192,128,64,0},{321,385,449,257,193,129,65,1},{322,386,..., dimensions={0} | all-to-all | bytes 131072 | tf_op jit(solution)/shard_map/cond/branch_0_fun/all_to_all | solution.py:18
  21.3 0.0 collective-permute-done.1
  21.3 1.0 %collective-permute-done = bf16[64,128]{1,0:T(8,128)(2,1)S(1)} collective-permute-done((bf16[64,128]{1,0:T(8,128)(2,1)S(1)}, bf16[64,128]{1,0:T(8,128)(2,1)S(1)}, u32[]{:S(2)}, u32[]{:S(2)}) %collective-permute-start) | collective-permute-done | bytes 16416 | tf_op jit(solution)/shard_map/ppermute | solution.py:76
  22.3 0.9 %broadcast_in_dim.10 = bf16[16,2,64,128]{3,2,1,0:T(8,128)(2,1)} broadcast(bf16[2,64,128]{2,1,0:T(8,128)(2,1)S(1)} %pad_maximum_fusion), dimensions={1,2,3} | broadcast | bytes 557056 | tf_op jit(solution)/shard_map/broadcast_in_dim | solution.py:17
  23.2 9.1 %all-to-all-start.2 = ((bf16[16,2,64,128]{3,2,1,0:T(8,128)(2,1)}), bf16[16,2,64,128]{3,2,1,0:T(8,128)(2,1)S(1)}, u32[]{:S(2)}, u32[]{:S(2)}) async-start(bf16[16,2,64,128]{3,2,1,0:T(8,128)(2,1)} %broadcast_in_dim.10), calls=%async_computation.2 | async-start | bytes 1048576 | tf_op jit(solution)/shard_map/all_to_all | solution.py:18
  32.3 1.9 %all-gather = bf16[8,32,256]{2,1,0:T(8,128)(2,1)S(1)} all-gather(bf16[8,16,256]{2,1,0:T(8,128)(2,1)S(1)} %get-tuple-element.21), channel_id=2, replica_groups=mesh['z_lo'=8,'core'=2,'z_hi'=2,'y'=4,'x'=4] {'core'}, dimensions={1}, use_global_device_ids=true | all-gather | bytes 196608 | tf_op jit(solution)/shard_map/all_gather | solution.py:78
  34.1 3.3 %all-to-all-done.2.int_ref = bf16[16,2,64,128]{3,2,1,0:T(8,128)(2,1)S(1)} async-done(((bf16[16,2,64,128]{3,2,1,0:T(8,128)(2,1)}), bf16[16,2,64,128]{3,2,1,0:T(8,128)(2,1)S(1)}, u32[]{:S(2)}, u32[]{:S(2)}) %all-to-all-start.2) | async-done | bytes 524320 | tf_op jit(solution)/shard_map/all_to_all | solution.py:18
  37.4 0.0 copy-done
  37.4 1.3 %shard_map.37 = f32[256,1024]{1,0:T(8,128)} custom-call(bf16[8,2,16,256]{3,2,1,0:T(8,128)(2,1)S(1)} %bitcast.9, bf16[16,2,64,128]{3,2,1,0:T(8,128)(2,1)S(1)} %all-to-all-done.2.int_ref, f32[256,1024]{1,0:T(8,128)S(1)} %copy-done), custom_call_target="tpu_custom_call" | custom-call | flops 134217728 | bytes 2097152 | tf_op jit(solution)/shard_map/pallas_call | solution.py:49
  (5 shorter events, 0.1 us)
Async XLA Ops:
  0.0 6.5 %copy-start.1 = (bf16[256,16]{0,1:T(8,128)(2,1)S(1)}, bf16[256,16]{0,1:T(8,128)(2,1)}, u32[]{:S(2)}) copy-start(bf16[256,16]{0,1:T(8,128)(2,1)} %param.7) | copy-start | bytes 24580
  0.0 21.3 %collective-permute-start.1 = (bf16[64,128]{1,0:T(8,128)(2,1)}, bf16[64,128]{1,0:T(8,128)(2,1)S(1)}, u32[]{:S(2)}, u32[]{:S(2)}) collective-permute-start(bf16[64,128]{1,0:T(8,128)(2,1)} %bitcast.12), channel_id=1, source_target_pairs={{16,0},{17,1},{18,2},{19,3},{20,4},{21,5},{22,6},{23,7},{24,8},{25... | collective-permute-start | bytes 49160 | tf_op jit(solution)/shard_map/ppermute | solution.py:68
  6.5 0.8 %copy-start.2 = (bf16[128,64]{0,1:T(8,128)(2,1)S(1)}, bf16[128,64]{0,1:T(8,128)(2,1)}, u32[]{:S(2)}) copy-start(bf16[128,64]{0,1:T(8,128)(2,1)} %param.8) | copy-start | bytes 49156
  7.2 30.2 %copy-start = (f32[256,1024]{1,0:T(8,128)S(1)}, f32[256,1024]{1,0:T(8,128)}, u32[]{:S(2)}) copy-start(f32[256,1024]{1,0:T(8,128)} %old_ref.1) | copy-start | bytes 3145732
  7.2 15.0 %collective-permute-start = (bf16[64,128]{1,0:T(8,128)(2,1)S(1)}, bf16[64,128]{1,0:T(8,128)(2,1)S(1)}, u32[]{:S(2)}, u32[]{:S(2)}) collective-permute-start(bf16[64,128]{1,0:T(8,128)(2,1)S(1)} %bitcast.13), channel_id=1, source_target_pairs={{0,16},{1,17},{2,18},{3,19},{4,20},{5,21},{6,22},{7,23},{8,24},{9,... | collective-permute-start | bytes 49160 | tf_op jit(solution)/shard_map/ppermute | solution.py:76
  23.2 14.2 %all-to-all-start.2 = ((bf16[16,2,64,128]{3,2,1,0:T(8,128)(2,1)}), bf16[16,2,64,128]{3,2,1,0:T(8,128)(2,1)S(1)}, u32[]{:S(2)}, u32[]{:S(2)}) async-start(bf16[16,2,64,128]{3,2,1,0:T(8,128)(2,1)} %broadcast_in_dim.10), calls=%async_computation.2 | async-start | bytes 1048576 | tf_op jit(solution)/shard_map/all_to_all | solution.py:18

commit v4 on v3

--- a/solution.py
+++ b/solution.py
@@ -9,7 +9,7 @@
 ROW = ("z_lo", "core")
 COL = ("z_hi", "y")
 PLANE = ("y", "x")
-Z_ORDER = (5, 6, 7, 4, 3, 2, 1, 0)
+Z_ORDER = (6, 7, 5, 4, 3, 2, 1, 0)
 PLANE_ORDER = tuple((10 + i) % (Y * X) for i in range(Y * X))
 
 

time: 39 us -> 38.6 us (0.990)
  blocking collectives: 14.5 us -> 15.5 us
  starting transfers between devices: 16.9 us -> 15.9 us
  waiting for transfers between devices: 4.28 us -> 3.8 us
    all_to_all x1, blocking collectives: 12.6 us -> 13.7 us  [spread(): return lax.all_to_all(copies, axes, 0, 0, axis_index_groups=[list(order)])]
    all_to_all x1, starting transfers between devices: 9.05 us -> 8.07 us  [spread(): return lax.all_to_all(copies, axes, 0, 0, axis_index_groups=[list(order)])]
    ppermute x1, waiting for transfers between devices: 1.01 us -> 0.34 us  [per_device(): up = lax.ppermute(again, 'z_hi', [(0, 1)])]
where the time goes in v4:
time: 38.6 us; the launch traced here: 38.3 us
  starting transfers between devices  15.9 us (41%)
  blocking collectives  15.5 us (40%)
  waiting for transfers between devices  3.8 us (10%)
  local copies, waits for them, and re-layouts  1.65 us (4%)
  Pallas kernels  1.26 us (3%)
    all_to_all x1, blocking collectives, spread(): return lax.all_to_all(copies, axes, 0, 0, axis_index_groups=[list(order)])  13.7 us
    all_to_all x1, starting transfers between devices, spread(): return lax.all_to_all(copies, axes, 0, 0, axis_index_groups=[list(order)])  8.07 us
    ppermute x1, starting transfers between devices, per_device(): down = lax.ppermute(mine, 'z_hi', [(1, 0)])  6.45 us
    all_to_all x1, waiting for transfers between devices, spread(): return lax.all_to_all(copies, axes, 0, 0, axis_index_groups=[list(order)])  3.46 us
    all_gather x1, blocking collectives, per_device(): amp_full = lax.all_gather(near, 'core', axis=1)  1.89 us
    ppermute x1, starting transfers between devices, per_device(): up = lax.ppermute(again, 'z_hi', [(0, 1)])  1.41 us
    pallas_call x1, Pallas kernels, add_ladder(): pl.pallas_call(ladder_kernel, out_shape=jax.ShapeDtypeStruct(old.shape, o...  1.26 us
    broadcast_in_dim x2, local copies, waits for them, and re-layouts, spread(): copies = jnp.broadcast_to(block[None], (len(order),) + block.shape)  0.92 us
  transfers between devices with their start and end apart: 3, of which 2 were waited for; matrix products, arithmetic and copies ran while one was open for 0% of the time, Pallas kernels for 0%

profile of v4, /device:TPU:480, one launch (start us, length us, event | category | flops | bytes accessed | tf_op | source)
XLA Modules:
  0.0 38.3 jit_solution(9521340818709372506)
XLA Ops:
  0.0 0.0 copy-start.1
  0.0 6.5 %collective-permute-start.1 = (bf16[64,128]{1,0:T(8,128)(2,1)}, bf16[64,128]{1,0:T(8,128)(2,1)S(1)}, u32[]{:S(2)}, u32[]{:S(2)}) collective-permute-start(bf16[64,128]{1,0:T(8,128)(2,1)} %bitcast.12), channel_id=1, source_target_pairs={{16,0},{17,1},{18,2},{19,3},{20,4},{21,5},{22,6},{23,7},{24,8},{25... | collective-permute-start | bytes 49160 | tf_op jit(solution)/shard_map/ppermute | solution.py:68
  6.5 0.0 copy-done.1
  6.5 0.0 copy-start.2
  6.5 0.7 %copy-done.2 = bf16[128,64]{0,1:T(8,128)(2,1)S(1)} copy-done((bf16[128,64]{0,1:T(8,128)(2,1)S(1)}, bf16[128,64]{0,1:T(8,128)(2,1)}, u32[]{:S(2)}) %copy-start.2) | copy-done | bytes 16408
  7.2 0.0 copy-start
  7.2 1.4 %collective-permute-start = (bf16[64,128]{1,0:T(8,128)(2,1)S(1)}, bf16[64,128]{1,0:T(8,128)(2,1)S(1)}, u32[]{:S(2)}, u32[]{:S(2)}) collective-permute-start(bf16[64,128]{1,0:T(8,128)(2,1)S(1)} %bitcast.13), channel_id=1, source_target_pairs={{0,16},{1,17},{2,18},{3,19},{4,20},{5,21},{6,22},{7,23},{8,24},{9,... | collective-permute-start | bytes 49160 | tf_op jit(solution)/shard_map/ppermute | solution.py:76
  8.7 13.7 %conditional.3 = (bf16[8,16,256]{2,1,0:T(8,128)(2,1)S(1)}) conditional(s32[]{:T(128)} %convert_element_type.4, bf16[16,256]{1,0:T(8,128)(2,1)S(1)} %bitcast.11, bf16[8,16,256]{2,1,0:T(8,128)(2,1)S(1)} %get-tuple-element.20), branch_computations={%region_2.0_spmd, %region_3.0_spmd} | conditional | bytes 204808 | solution.py:77
  8.7 13.7 %all_to_all.14 = bf16[8,16,256]{2,1,0:T(8,128)(2,1)S(1)} all-to-all(bf16[8,16,256]{2,1,0:T(8,128)(2,1)S(1)} %broadcast_in_dim.8), channel_id=1, replica_groups={{384,448,320,256,192,128,64,0},{385,449,321,257,193,129,65,1},{386,450,..., dimensions={0} | all-to-all | bytes 131072 | tf_op jit(solution)/shard_map/cond/branch_0_fun/all_to_all | solution.py:18
  22.3 0.0 collective-permute-done.1
  22.3 0.3 collective-permute-done
  22.7 0.9 %broadcast_in_dim.10 = bf16[16,2,64,128]{3,2,1,0:T(8,128)(2,1)} broadcast(bf16[2,64,128]{2,1,0:T(8,128)(2,1)S(1)} %pad_maximum_fusion), dimensions={1,2,3} | broadcast | bytes 557056 | tf_op jit(solution)/shard_map/broadcast_in_dim | solution.py:17
  23.6 8.1 %all-to-all-start.2 = ((bf16[16,2,64,128]{3,2,1,0:T(8,128)(2,1)}), bf16[16,2,64,128]{3,2,1,0:T(8,128)(2,1)S(1)}, u32[]{:S(2)}, u32[]{:S(2)}) async-start(bf16[16,2,64,128]{3,2,1,0:T(8,128)(2,1)} %broadcast_in_dim.10), calls=%async_computation.2 | async-start | bytes 1048576 | tf_op jit(solution)/shard_map/all_to_all | solution.py:18
  31.7 1.9 %all-gather = bf16[8,32,256]{2,1,0:T(8,128)(2,1)S(1)} all-gather(bf16[8,16,256]{2,1,0:T(8,128)(2,1)S(1)} %get-tuple-element.21), channel_id=2, replica_groups=mesh['z_lo'=8,'core'=2,'z_hi'=2,'y'=4,'x'=4] {'core'}, dimensions={1}, use_global_device_ids=true | all-gather | bytes 196608 | tf_op jit(solution)/shard_map/all_gather | solution.py:78
  33.6 3.5 %all-to-all-done.2.int_ref = bf16[16,2,64,128]{3,2,1,0:T(8,128)(2,1)S(1)} async-done(((bf16[16,2,64,128]{3,2,1,0:T(8,128)(2,1)}), bf16[16,2,64,128]{3,2,1,0:T(8,128)(2,1)S(1)}, u32[]{:S(2)}, u32[]{:S(2)}) %all-to-all-start.2) | async-done | bytes 524320 | tf_op jit(solution)/shard_map/all_to_all | solution.py:18
  37.0 0.0 copy-done
  37.0 1.3 %shard_map.37 = f32[256,1024]{1,0:T(8,128)} custom-call(bf16[8,2,16,256]{3,2,1,0:T(8,128)(2,1)S(1)} %bitcast.9, bf16[16,2,64,128]{3,2,1,0:T(8,128)(2,1)S(1)} %all-to-all-done.2.int_ref, f32[256,1024]{1,0:T(8,128)S(1)} %copy-done), custom_call_target="tpu_custom_call" | custom-call | flops 134217728 | bytes 2097152 | tf_op jit(solution)/shard_map/pallas_call | solution.py:49
  (5 shorter events, 0.1 us)
Async XLA Ops:
  0.0 6.5 %copy-start.1 = (bf16[256,16]{0,1:T(8,128)(2,1)S(1)}, bf16[256,16]{0,1:T(8,128)(2,1)}, u32[]{:S(2)}) copy-start(bf16[256,16]{0,1:T(8,128)(2,1)} %param.7) | copy-start | bytes 24580
  0.0 22.3 %collective-permute-start.1 = (bf16[64,128]{1,0:T(8,128)(2,1)}, bf16[64,128]{1,0:T(8,128)(2,1)S(1)}, u32[]{:S(2)}, u32[]{:S(2)}) collective-permute-start(bf16[64,128]{1,0:T(8,128)(2,1)} %bitcast.12), channel_id=1, source_target_pairs={{16,0},{17,1},{18,2},{19,3},{20,4},{21,5},{22,6},{23,7},{24,8},{25... | collective-permute-start | bytes 49160 | tf_op jit(solution)/shard_map/ppermute | solution.py:68
  6.5 0.8 %copy-start.2 = (bf16[128,64]{0,1:T(8,128)(2,1)S(1)}, bf16[128,64]{0,1:T(8,128)(2,1)}, u32[]{:S(2)}) copy-start(bf16[128,64]{0,1:T(8,128)(2,1)} %param.8) | copy-start | bytes 49156
  7.2 29.8 %copy-start = (f32[256,1024]{1,0:T(8,128)S(1)}, f32[256,1024]{1,0:T(8,128)}, u32[]{:S(2)}) copy-start(f32[256,1024]{1,0:T(8,128)} %old_ref.1) | copy-start | bytes 3145732
  7.2 15.4 %collective-permute-start = (bf16[64,128]{1,0:T(8,128)(2,1)S(1)}, bf16[64,128]{1,0:T(8,128)(2,1)S(1)}, u32[]{:S(2)}, u32[]{:S(2)}) collective-permute-start(bf16[64,128]{1,0:T(8,128)(2,1)S(1)} %bitcast.13), channel_id=1, source_target_pairs={{0,16},{1,17},{2,18},{3,19},{4,20},{5,21},{6,22},{7,23},{8,24},{9,... | collective-permute-start | bytes 49160 | tf_op jit(solution)/shard_map/ppermute | solution.py:76
  23.6 13.4 %all-to-all-start.2 = ((bf16[16,2,64,128]{3,2,1,0:T(8,128)(2,1)}), bf16[16,2,64,128]{3,2,1,0:T(8,128)(2,1)S(1)}, u32[]{:S(2)}, u32[]{:S(2)}) async-start(bf16[16,2,64,128]{3,2,1,0:T(8,128)(2,1)} %broadcast_in_dim.10), calls=%async_computation.2 | async-start | bytes 1048576 | tf_op jit(solution)/shard_map/all_to_all | solution.py:18

commit v5 on v4

--- a/solution.py
+++ b/solution.py
@@ -62,6 +62,12 @@
     )(amp, integrals, old)
 
 
+def high_spread(amp):
+    order = (Z_ORDER[2], Z_ORDER[0], Z_ORDER[1]) + Z_ORDER[3:]
+    got = spread(amp, "z_lo", order)
+    return jnp.concatenate([got[1:3], got[:1], got[3:]])
+
+
 def per_device(amplitudes, integrals, old_residual):
     low = lax.axis_index("z_hi") == 0
     mine, amp = integrals.T, amplitudes.T
@@ -74,10 +80,14 @@
     )
     again, near = lax.optimization_barrier((mine, near))
     up = lax.ppermute(again, "z_hi", [(0, 1)])
-    near = lax.cond(low, lambda a, n: n, lambda a, n: spread(a, "z_lo", Z_ORDER), amp, near)
+    near = lax.cond(low, lambda a, n: n, lambda a, n: high_spread(a), amp, near)
     amp_full = lax.all_gather(near, "core", axis=1)
-    both = jnp.stack([jnp.where(low, mine, up), jnp.where(low, down, mine)])
-    integral_full = spread(both, PLANE, PLANE_ORDER)
+    slots = jnp.broadcast_to(mine[None, None], (Y * X, Z_HI) + mine.shape)
+    slots = lax.optimization_barrier(slots)
+    other = jnp.where(low, down, up)
+    other = jnp.broadcast_to(other[None, None], (Y * X, 1) + mine.shape)
+    slots = lax.dynamic_update_slice(slots, other, (0, jnp.where(low, 1, 0), 0, 0))
+    integral_full = lax.all_to_all(slots, PLANE, 0, 0, axis_index_groups=[list(PLANE_ORDER)])
     return add_ladder(amp_full, integral_full, old_residual)
 
 

time: 38.6 us -> 38.3 us (level)
  blocking collectives: 15.5 us -> 14.5 us
  local copies, waits for them, and re-layouts: 1.65 us -> 2.41 us
    all_to_all x1, blocking collectives: 13.7 us -> 12.6 us  [spread(): return lax.all_to_all(copies, axes, 0, 0, axis_index_groups=[list(order)])]
    broadcast_in_dim x0 -> x1, local copies, waits for them, and re-layouts: none -> 0.91 us  [per_device(): slots = jnp.broadcast_to(mine[None, None], (Y * X, Z_HI) + mine.shape)]
    broadcast_in_dim x2 -> x1, local copies, waits for them, and re-layouts: 0.92 us -> 0.01 us  [spread(): copies = jnp.broadcast_to(block[None], (len(order),) + block.shape)]
    dynamic_update_slice x0 -> x1, local copies, waits for them, and re-layouts: none -> 0.76 us  [per_device(): lax.dynamic_update_slice(slots, other, (0, jnp.where(low, 1, 0), 0, 0))]
  transfers between devices with their start and end apart: 3 -> 3, of which waited for: 2 -> 2; matrix products, arithmetic and copies ran while one was open for 0% -> 2% of each run, Pallas kernels for 0% -> 0%
where the time goes in v5:
time: 38.3 us; the launch traced here: 38 us
  starting transfers between devices  16 us (42%)
  blocking collectives  14.5 us (38%)
  waiting for transfers between devices  3.76 us (10%)
  local copies, waits for them, and re-layouts  2.41 us (6%)
  Pallas kernels  1.26 us (3%)
    all_to_all x1, blocking collectives, spread(): return lax.all_to_all(copies, axes, 0, 0, axis_index_groups=[list(order)])  12.6 us
    all_to_all x1, starting transfers between devices, per_device(): lax.all_to_all(slots, PLANE, 0, 0, axis_index_groups=[list(PLANE_ORDER)])  8.22 us
    ppermute x1, starting transfers between devices, per_device(): down = lax.ppermute(mine, 'z_hi', [(1, 0)])  6.45 us
    all_to_all x1, waiting for transfers between devices, per_device(): lax.all_to_all(slots, PLANE, 0, 0, axis_index_groups=[list(PLANE_ORDER)])  3.31 us
    all_gather x1, blocking collectives, per_device(): amp_full = lax.all_gather(near, 'core', axis=1)  1.89 us
    ppermute x1, starting transfers between devices, per_device(): up = lax.ppermute(again, 'z_hi', [(0, 1)])  1.28 us
    pallas_call x1, Pallas kernels, add_ladder(): pl.pallas_call(ladder_kernel, out_shape=jax.ShapeDtypeStruct(old.shape, o...  1.26 us
    broadcast_in_dim x1, local copies, waits for them, and re-layouts, per_device(): slots = jnp.broadcast_to(mine[None, None], (Y * X, Z_HI) + mine.shape)  0.91 us
  transfers between devices with their start and end apart: 3, of which 2 were waited for; matrix products, arithmetic and copies ran while one was open for 2% of the time, Pallas kernels for 0%

profile of v5, /device:TPU:480, one launch (start us, length us, event | category | flops | bytes accessed | tf_op | source)
XLA Modules:
  0.0 38.0 jit_solution(10220062916850661796)
XLA Ops:
  0.0 0.0 copy-start.1
  0.0 6.5 %collective-permute-start = (bf16[64,128]{1,0:T(8,128)(2,1)}, bf16[64,128]{1,0:T(8,128)(2,1)S(1)}, u32[]{:S(2)}, u32[]{:S(2)}) collective-permute-start(bf16[64,128]{1,0:T(8,128)(2,1)} %bitcast.6), channel_id=1, source_target_pairs={{16,0},{17,1},{18,2},{19,3},{20,4},{21,5},{22,6},{23,7},{24,8},{25... | collective-permute-start | bytes 49160 | tf_op jit(solution)/shard_map/ppermute | solution.py:74
  6.5 0.0 copy-done.1
  6.5 0.0 copy-start.2
  6.5 0.7 %copy-done.2 = bf16[128,64]{0,1:T(8,128)(2,1)S(1)} copy-done((bf16[128,64]{0,1:T(8,128)(2,1)S(1)}, bf16[128,64]{0,1:T(8,128)(2,1)}, u32[]{:S(2)}) %copy-start.2) | copy-done | bytes 16408
  7.2 1.3 %collective-permute-start.1 = (bf16[64,128]{1,0:T(8,128)(2,1)S(1)}, bf16[64,128]{1,0:T(8,128)(2,1)S(1)}, u32[]{:S(2)}, u32[]{:S(2)}) collective-permute-start(bf16[64,128]{1,0:T(8,128)(2,1)S(1)} %bitcast.7), channel_id=1, source_target_pairs={{0,16},{1,17},{2,18},{3,19},{4,20},{5,21},{6,22},{7,23},{8,24},{9,... | collective-permute-start | bytes 49160 | tf_op jit(solution)/shard_map/ppermute | solution.py:82
  8.5 12.6 %conditional.3 = (bf16[8,16,256]{2,1,0:T(8,128)(2,1)S(1)}) conditional(s32[]{:T(128)} %convert_element_type.4, bf16[16,256]{1,0:T(8,128)(2,1)S(1)} %bitcast.5, bf16[8,16,256]{2,1,0:T(8,128)(2,1)S(1)} %get-tuple-element.18), branch_computations={%region_2.0_spmd, %region_3.0_spmd} | conditional | flops 65536 | bytes 466952 | solution.py:83
  8.6 12.6 %all_to_all.14 = bf16[8,16,256]{2,1,0:T(8,128)(2,1)S(1)} all-to-all(bf16[8,16,256]{2,1,0:T(8,128)(2,1)S(1)} %broadcast_in_dim.9), channel_id=1, replica_groups={{320,384,448,256,192,128,64,0},{321,385,449,257,193,129,65,1},{322,386,..., dimensions={0} | all-to-all | bytes 131072 | tf_op jit(solution)/shard_map/cond/branch_0_fun/all_to_all | solution.py:18
  21.2 0.0 copy-start
  21.2 0.9 %broadcast_in_dim.16 = bf16[16,2,64,128]{3,2,1,0:T(8,128)(2,1)} broadcast(bf16[64,128]{1,0:T(8,128)(2,1)S(1)} %bitcast.8), dimensions={2,3} | broadcast | bytes 540672 | tf_op jit(solution)/shard_map/broadcast_in_dim | solution.py:85
  22.1 0.0 collective-permute-done
  22.1 0.4 %collective-permute-done.1 = bf16[64,128]{1,0:T(8,128)(2,1)S(1)} collective-permute-done((bf16[64,128]{1,0:T(8,128)(2,1)S(1)}, bf16[64,128]{1,0:T(8,128)(2,1)S(1)}, u32[]{:S(2)}, u32[]{:S(2)}) %collective-permute-start.1) | collective-permute-done | bytes 16416 | tf_op jit(solution)/shard_map/ppermute | solution.py:82
  22.6 0.8 %broadcast_dynamic-update-slice_fusion = bf16[16,2,64,128]{3,2,1,0:T(8,128)(2,1)} fusion(bf16[16,2,64,128]{3,2,1,0:T(8,128)(2,1)} %broadcast_in_dim.16, s32[]{:T(128)S(6)} %select_n.15, bf16[64,128]{1,0:T(8,128)(2,1)S(1)} %broadcast_select_fusion), kind=kLoop, calls=%fused_computation.1 | loop fusion | bytes 278532 | tf_op jit(solution)/shard_map/dynamic_update_slice | solution.py:89
  23.3 8.2 %all-to-all-start.2 = ((bf16[16,2,64,128]{3,2,1,0:T(8,128)(2,1)}), bf16[16,2,64,128]{3,2,1,0:T(8,128)(2,1)S(1)}, u32[]{:S(2)}, u32[]{:S(2)}) async-start(bf16[16,2,64,128]{3,2,1,0:T(8,128)(2,1)} %broadcast_dynamic-update-slice_fusion), calls=%async_computation.2 | async-start | bytes 1048576 | tf_op jit(solution)/shard_map/all_to_all | solution.py:90
  31.5 1.9 %all-gather = bf16[8,32,256]{2,1,0:T(8,128)(2,1)S(1)} all-gather(bf16[8,16,256]{2,1,0:T(8,128)(2,1)S(1)} %get-tuple-element.19), channel_id=2, replica_groups=mesh['z_lo'=8,'core'=2,'z_hi'=2,'y'=4,'x'=4] {'core'}, dimensions={1}, use_global_device_ids=true | all-gather | bytes 196608 | tf_op jit(solution)/shard_map/all_gather | solution.py:84
  33.4 3.3 %all-to-all-done.2.int_ref = bf16[16,2,64,128]{3,2,1,0:T(8,128)(2,1)S(1)} async-done(((bf16[16,2,64,128]{3,2,1,0:T(8,128)(2,1)}), bf16[16,2,64,128]{3,2,1,0:T(8,128)(2,1)S(1)}, u32[]{:S(2)}, u32[]{:S(2)}) %all-to-all-start.2) | async-done | bytes 524320 | tf_op jit(solution)/shard_map/all_to_all | solution.py:90
  36.7 0.0 copy-done
  36.7 1.3 %shard_map.37 = f32[256,1024]{1,0:T(8,128)} custom-call(bf16[8,2,16,256]{3,2,1,0:T(8,128)(2,1)S(1)} %bitcast.3, bf16[16,2,64,128]{3,2,1,0:T(8,128)(2,1)S(1)} %all-to-all-done.2.int_ref, f32[256,1024]{1,0:T(8,128)S(1)} %copy-done), custom_call_target="tpu_custom_call" | custom-call | flops 134217728 | bytes 2097152 | tf_op jit(solution)/shard_map/pallas_call | solution.py:49
  (8 shorter events, 0.1 us)
Async XLA Ops:
  0.0 6.5 %copy-start.1 = (bf16[256,16]{0,1:T(8,128)(2,1)S(1)}, bf16[256,16]{0,1:T(8,128)(2,1)}, u32[]{:S(2)}) copy-start(bf16[256,16]{0,1:T(8,128)(2,1)} %param.7) | copy-start | bytes 24580
  0.0 22.1 %collective-permute-start = (bf16[64,128]{1,0:T(8,128)(2,1)}, bf16[64,128]{1,0:T(8,128)(2,1)S(1)}, u32[]{:S(2)}, u32[]{:S(2)}) collective-permute-start(bf16[64,128]{1,0:T(8,128)(2,1)} %bitcast.6), channel_id=1, source_target_pairs={{16,0},{17,1},{18,2},{19,3},{20,4},{21,5},{22,6},{23,7},{24,8},{25... | collective-permute-start | bytes 49160 | tf_op jit(solution)/shard_map/ppermute | solution.py:74
  6.5 0.8 %copy-start.2 = (bf16[128,64]{0,1:T(8,128)(2,1)S(1)}, bf16[128,64]{0,1:T(8,128)(2,1)}, u32[]{:S(2)}) copy-start(bf16[128,64]{0,1:T(8,128)(2,1)} %param.8) | copy-start | bytes 49156
  7.2 15.3 %collective-permute-start.1 = (bf16[64,128]{1,0:T(8,128)(2,1)S(1)}, bf16[64,128]{1,0:T(8,128)(2,1)S(1)}, u32[]{:S(2)}, u32[]{:S(2)}) collective-permute-start(bf16[64,128]{1,0:T(8,128)(2,1)S(1)} %bitcast.7), channel_id=1, source_target_pairs={{0,16},{1,17},{2,18},{3,19},{4,20},{5,21},{6,22},{7,23},{8,24},{9,... | collective-permute-start | bytes 49160 | tf_op jit(solution)/shard_map/ppermute | solution.py:82
  21.2 15.6 %copy-start = (f32[256,1024]{1,0:T(8,128)S(1)}, f32[256,1024]{1,0:T(8,128)}, u32[]{:S(2)}) copy-start(f32[256,1024]{1,0:T(8,128)} %old_ref.1) | copy-start | bytes 3145732
  23.3 13.4 %all-to-all-start.2 = ((bf16[16,2,64,128]{3,2,1,0:T(8,128)(2,1)}), bf16[16,2,64,128]{3,2,1,0:T(8,128)(2,1)S(1)}, u32[]{:S(2)}, u32[]{:S(2)}) async-start(bf16[16,2,64,128]{3,2,1,0:T(8,128)(2,1)} %broadcast_dynamic-update-slice_fusion), calls=%async_computation.2 | async-start | bytes 1048576 | tf_op jit(solution)/shard_map/all_to_all | solution.py:90

commit v6 on v5

--- a/solution.py
+++ b/solution.py
@@ -80,10 +80,18 @@
     )
     again, near = lax.optimization_barrier((mine, near))
     up = lax.ppermute(again, "z_hi", [(0, 1)])
-    near = lax.cond(low, lambda a, n: n, lambda a, n: high_spread(a), amp, near)
+    def filled(block):
+        return jnp.broadcast_to(block[None, None], (Y * X, Z_HI) + block.shape)
+
+    near, slots = lax.cond(
+        low,
+        lambda a, m, n: (n, filled(m)),
+        lambda a, m, n: (high_spread(a), filled(m)),
+        amp,
+        mine,
+        near,
+    )
     amp_full = lax.all_gather(near, "core", axis=1)
-    slots = jnp.broadcast_to(mine[None, None], (Y * X, Z_HI) + mine.shape)
-    slots = lax.optimization_barrier(slots)
     other = jnp.where(low, down, up)
     other = jnp.broadcast_to(other[None, None], (Y * X, 1) + mine.shape)
     slots = lax.dynamic_update_slice(slots, other, (0, jnp.where(low, 1, 0), 0, 0))

time: 38.3 us -> 38.6 us (level)
  blocking collectives: 14.5 us -> 15 us
    broadcast_in_dim x1, local copies, waits for them, and re-layouts: 0.91 us -> 1.63 us  [filled(): return jnp.broadcast_to(block[None, None], (Y * X, Z_HI) + block.shape)]
    unnamed x6 -> x4, local copies, waits for them, and re-layouts: 0.72 us -> 0.01 us
    all_to_all x1, blocking collectives: 12.6 us -> 13.1 us  [spread(): return lax.all_to_all(copies, axes, 0, 0, axis_index_groups=[list(order)])]
  transfers between devices with their start and end apart: 3 -> 3, of which waited for: 2 -> 2; matrix products, arithmetic and copies ran while one was open for 2% -> 4% of each run, Pallas kernels for 0% -> 0%
where the time goes in v6:
time: 38.6 us; the launch traced here: 38.2 us
  starting transfers between devices  16 us (41%)
  blocking collectives  15 us (39%)
  waiting for transfers between devices  3.42 us (9%)
  local copies, waits for them, and re-layouts  2.42 us (6%)
  Pallas kernels  1.26 us (3%)
    all_to_all x1, blocking collectives, spread(): return lax.all_to_all(copies, axes, 0, 0, axis_index_groups=[list(order)])  13.1 us
    all_to_all x1, starting transfers between devices, per_device(): lax.all_to_all(slots, PLANE, 0, 0, axis_index_groups=[list(PLANE_ORDER)])  8.27 us
    ppermute x1, starting transfers between devices, per_device(): down = lax.ppermute(mine, 'z_hi', [(1, 0)])  6.45 us
    all_to_all x1, waiting for transfers between devices, per_device(): lax.all_to_all(slots, PLANE, 0, 0, axis_index_groups=[list(PLANE_ORDER)])  3.27 us
    all_gather x1, blocking collectives, per_device(): amp_full = lax.all_gather(near, 'core', axis=1)  1.89 us
    broadcast_in_dim x1, local copies, waits for them, and re-layouts, filled(): return jnp.broadcast_to(block[None, None], (Y * X, Z_HI) + block.shape)  1.63 us
    ppermute x1, starting transfers between devices, per_device(): up = lax.ppermute(again, 'z_hi', [(0, 1)])  1.29 us
    pallas_call x1, Pallas kernels, add_ladder(): pl.pallas_call(ladder_kernel, out_shape=jax.ShapeDtypeStruct(old.shape, o...  1.26 us
  transfers between devices with their start and end apart: 3, of which 2 were waited for; matrix products, arithmetic and copies ran while one was open for 4% of the time, Pallas kernels for 0%

profile of v6, /device:TPU:480, one launch (start us, length us, event | category | flops | bytes accessed | tf_op | source)
XLA Modules:
  0.0 38.2 jit_solution(7876154608767520871)
XLA Ops:
  0.0 0.0 copy-start.1
  0.0 6.5 %collective-permute-start = (bf16[64,128]{1,0:T(8,128)(2,1)}, bf16[64,128]{1,0:T(8,128)(2,1)S(1)}, u32[]{:S(2)}, u32[]{:S(2)}) collective-permute-start(bf16[64,128]{1,0:T(8,128)(2,1)} %bitcast.1), channel_id=1, source_target_pairs={{16,0},{17,1},{18,2},{19,3},{20,4},{21,5},{22,6},{23,7},{24,8},{25... | collective-permute-start | bytes 49160 | tf_op jit(solution)/shard_map/ppermute | solution.py:74
  6.5 0.0 copy-done.1
  6.5 1.3 %collective-permute-start.1 = (bf16[64,128]{1,0:T(8,128)(2,1)}, bf16[64,128]{1,0:T(8,128)(2,1)S(1)}, u32[]{:S(2)}, u32[]{:S(2)}) collective-permute-start(bf16[64,128]{1,0:T(8,128)(2,1)} %bitcast.1), channel_id=1, source_target_pairs={{0,16},{1,17},{2,18},{3,19},{4,20},{5,21},{6,22},{7,23},{8,24},{9,... | collective-permute-start | bytes 49160 | tf_op jit(solution)/shard_map/ppermute | solution.py:82
  7.8 14.8 %conditional.3 = (bf16[8,16,256]{2,1,0:T(8,128)(2,1)S(1)}, bf16[16,2,64,128]{3,2,1,0:T(8,128)(2,1)}) conditional(s32[]{:T(128)} %convert_element_type.4, (bf16[16,256]{1,0:T(8,128)(2,1)S(1)}, bf16[64,128]{1,0:T(8,128)(2,1)}) %tuple.28, (bf16[64,128]{1,0:T(8,128)(2,1)}, bf16[8,16,256]{2,1,0:T(8,128)(2,1)S(1)}) %tuple.23), branch_computations={%region_2.0_spmd, %region_3.0_spmd} | conditional | flops 65536 | bytes 1007632 | solution.py:86
  7.9 13.1 %all_to_all.14 = bf16[8,16,256]{2,1,0:T(8,128)(2,1)S(1)} all-to-all(bf16[8,16,256]{2,1,0:T(8,128)(2,1)S(1)} %broadcast_in_dim.10), channel_id=1, replica_groups={{320,384,448,256,192,128,64,0},{321,385,449,257,193,129,65,1},{322,386,..., dimensions={0} | all-to-all | bytes 131072 | tf_op jit(solution)/shard_map/cond/branch_0_fun/all_to_all | solution.py:18
  21.0 1.6 %broadcast_in_dim.11 = bf16[16,2,64,128]{3,2,1,0:T(8,128)(2,1)} broadcast(bf16[64,128]{1,0:T(8,128)(2,1)} %get-tuple-element.18), dimensions={2,3} | broadcast | bytes 540672 | tf_op jit(solution)/shard_map/cond/branch_0_fun/broadcast_in_dim | solution.py:84
  22.6 0.0 copy-start
  22.6 0.0 collective-permute-done
  22.6 0.1 collective-permute-done.1
  22.8 0.8 %broadcast_dynamic-update-slice_fusion = bf16[16,2,64,128]{3,2,1,0:T(8,128)(2,1)} fusion(bf16[16,2,64,128]{3,2,1,0:T(8,128)(2,1)} %get-tuple-element.27, s32[]{:T(128)S(6)} %select_n.15, bf16[64,128]{1,0:T(8,128)(2,1)S(1)} %broadcast_select_fusion), kind=kLoop, calls=%fused_computation.1 | loop fusion | bytes 278532 | tf_op jit(solution)/shard_map/dynamic_update_slice | solution.py:97
  23.5 8.3 %all-to-all-start.2 = ((bf16[16,2,64,128]{3,2,1,0:T(8,128)(2,1)}), bf16[16,2,64,128]{3,2,1,0:T(8,128)(2,1)S(1)}, u32[]{:S(2)}, u32[]{:S(2)}) async-start(bf16[16,2,64,128]{3,2,1,0:T(8,128)(2,1)} %broadcast_dynamic-update-slice_fusion), calls=%async_computation.2 | async-start | bytes 1048576 | tf_op jit(solution)/shard_map/all_to_all | solution.py:98
  31.8 1.9 %all-gather = bf16[8,32,256]{2,1,0:T(8,128)(2,1)S(1)} all-gather(bf16[8,16,256]{2,1,0:T(8,128)(2,1)S(1)} %get-tuple-element.26), channel_id=2, replica_groups=mesh['z_lo'=8,'core'=2,'z_hi'=2,'y'=4,'x'=4] {'core'}, dimensions={1}, use_global_device_ids=true | all-gather | bytes 196608 | tf_op jit(solution)/shard_map/all_gather | solution.py:94
  33.7 3.3 %all-to-all-done.2.int_ref = bf16[16,2,64,128]{3,2,1,0:T(8,128)(2,1)S(1)} async-done(((bf16[16,2,64,128]{3,2,1,0:T(8,128)(2,1)}), bf16[16,2,64,128]{3,2,1,0:T(8,128)(2,1)S(1)}, u32[]{:S(2)}, u32[]{:S(2)}) %all-to-all-start.2) | async-done | bytes 524320 | tf_op jit(solution)/shard_map/all_to_all | solution.py:98
  36.9 0.0 copy-done
  36.9 1.3 %shard_map.37 = f32[256,1024]{1,0:T(8,128)} custom-call(bf16[8,2,16,256]{3,2,1,0:T(8,128)(2,1)S(1)} %bitcast.3, bf16[16,2,64,128]{3,2,1,0:T(8,128)(2,1)S(1)} %all-to-all-done.2.int_ref, f32[256,1024]{1,0:T(8,128)S(1)} %copy-done), custom_call_target="tpu_custom_call" | custom-call | flops 134217728 | bytes 2097152 | tf_op jit(solution)/shard_map/pallas_call | solution.py:49
  (8 shorter events, 0.1 us)
Async XLA Ops:
  0.0 6.5 %copy-start.1 = (bf16[256,16]{0,1:T(8,128)(2,1)S(1)}, bf16[256,16]{0,1:T(8,128)(2,1)}, u32[]{:S(2)}) copy-start(bf16[256,16]{0,1:T(8,128)(2,1)} %param.7) | copy-start | bytes 24580
  0.0 22.6 %collective-permute-start = (bf16[64,128]{1,0:T(8,128)(2,1)}, bf16[64,128]{1,0:T(8,128)(2,1)S(1)}, u32[]{:S(2)}, u32[]{:S(2)}) collective-permute-start(bf16[64,128]{1,0:T(8,128)(2,1)} %bitcast.1), channel_id=1, source_target_pairs={{16,0},{17,1},{18,2},{19,3},{20,4},{21,5},{22,6},{23,7},{24,8},{25... | collective-permute-start | bytes 49160 | tf_op jit(solution)/shard_map/ppermute | solution.py:74
  6.5 16.2 %collective-permute-start.1 = (bf16[64,128]{1,0:T(8,128)(2,1)}, bf16[64,128]{1,0:T(8,128)(2,1)S(1)}, u32[]{:S(2)}, u32[]{:S(2)}) collective-permute-start(bf16[64,128]{1,0:T(8,128)(2,1)} %bitcast.1), channel_id=1, source_target_pairs={{0,16},{1,17},{2,18},{3,19},{4,20},{5,21},{6,22},{7,23},{8,24},{9,... | collective-permute-start | bytes 49160 | tf_op jit(solution)/shard_map/ppermute | solution.py:82
  22.6 14.4 %copy-start = (f32[256,1024]{1,0:T(8,128)S(1)}, f32[256,1024]{1,0:T(8,128)}, u32[]{:S(2)}) copy-start(f32[256,1024]{1,0:T(8,128)} %old_ref.1) | copy-start | bytes 3145732
  23.5 13.4 %all-to-all-start.2 = ((bf16[16,2,64,128]{3,2,1,0:T(8,128)(2,1)}), bf16[16,2,64,128]{3,2,1,0:T(8,128)(2,1)S(1)}, u32[]{:S(2)}, u32[]{:S(2)}) async-start(bf16[16,2,64,128]{3,2,1,0:T(8,128)(2,1)} %broadcast_dynamic-update-slice_fusion), calls=%async_computation.2 | async-start | bytes 1048576 | tf_op jit(solution)/shard_map/all_to_all | solution.py:98

commit v7 on v5

--- a/solution.py
+++ b/solution.py
@@ -9,7 +9,7 @@
 ROW = ("z_lo", "core")
 COL = ("z_hi", "y")
 PLANE = ("y", "x")
-Z_ORDER = (6, 7, 5, 4, 3, 2, 1, 0)
+Z_ORDER = (5, 6, 7, 4, 3, 2, 1, 0)
 PLANE_ORDER = tuple((10 + i) % (Y * X) for i in range(Y * X))
 
 
@@ -62,12 +62,6 @@
     )(amp, integrals, old)
 
 
-def high_spread(amp):
-    order = (Z_ORDER[2], Z_ORDER[0], Z_ORDER[1]) + Z_ORDER[3:]
-    got = spread(amp, "z_lo", order)
-    return jnp.concatenate([got[1:3], got[:1], got[3:]])
-
-
 def per_device(amplitudes, integrals, old_residual):
     low = lax.axis_index("z_hi") == 0
     mine, amp = integrals.T, amplitudes.T
@@ -80,7 +74,7 @@
     )
     again, near = lax.optimization_barrier((mine, near))
     up = lax.ppermute(again, "z_hi", [(0, 1)])
-    near = lax.cond(low, lambda a, n: n, lambda a, n: high_spread(a), amp, near)
+    near = lax.cond(low, lambda a, n: n, lambda a, n: spread(a, "z_lo", Z_ORDER), amp, near)
     amp_full = lax.all_gather(near, "core", axis=1)
     slots = jnp.broadcast_to(mine[None, None], (Y * X, Z_HI) + mine.shape)
     slots = lax.optimization_barrier(slots)

time: 38.3 us -> 38.7 us (1.010)
  starting transfers between devices: 16 us -> 16.8 us
  waiting for transfers between devices: 3.76 us -> 3.36 us
    all_to_all x1, starting transfers between devices: 8.22 us -> 9.05 us  [per_device(): lax.all_to_all(slots, PLANE, 0, 0, axis_index_groups=[list(PLANE_ORDER)])]
where the time goes in v7:
time: 38.7 us; the launch traced here: 38.4 us
  starting transfers between devices  16.8 us (43%)
  blocking collectives  14.5 us (37%)
  waiting for transfers between devices  3.36 us (9%)
  local copies, waits for them, and re-layouts  2.4 us (6%)
  Pallas kernels  1.26 us (3%)
    all_to_all x1, blocking collectives, spread(): return lax.all_to_all(copies, axes, 0, 0, axis_index_groups=[list(order)])  12.6 us
    all_to_all x1, starting transfers between devices, per_device(): lax.all_to_all(slots, PLANE, 0, 0, axis_index_groups=[list(PLANE_ORDER)])  9.05 us
    ppermute x1, starting transfers between devices, per_device(): down = lax.ppermute(mine, 'z_hi', [(1, 0)])  6.45 us
    all_to_all x1, waiting for transfers between devices, per_device(): lax.all_to_all(slots, PLANE, 0, 0, axis_index_groups=[list(PLANE_ORDER)])  3.27 us
    all_gather x1, blocking collectives, per_device(): amp_full = lax.all_gather(near, 'core', axis=1)  1.89 us
    ppermute x1, starting transfers between devices, per_device(): up = lax.ppermute(again, 'z_hi', [(0, 1)])  1.28 us
    pallas_call x1, Pallas kernels, add_ladder(): pl.pallas_call(ladder_kernel, out_shape=jax.ShapeDtypeStruct(old.shape, o...  1.26 us
    broadcast_in_dim x1, local copies, waits for them, and re-layouts, per_device(): slots = jnp.broadcast_to(mine[None, None], (Y * X, Z_HI) + mine.shape)  0.91 us
  transfers between devices with their start and end apart: 3, of which 2 were waited for; matrix products, arithmetic and copies ran while one was open for 2% of the time, Pallas kernels for 0%

profile of v7, /device:TPU:480, one launch (start us, length us, event | category | flops | bytes accessed | tf_op | source)
XLA Modules:
  0.0 38.4 jit_solution(17789787995009804511)
XLA Ops:
  0.0 0.0 copy-start.1
  0.0 6.5 %collective-permute-start = (bf16[64,128]{1,0:T(8,128)(2,1)}, bf16[64,128]{1,0:T(8,128)(2,1)S(1)}, u32[]{:S(2)}, u32[]{:S(2)}) collective-permute-start(bf16[64,128]{1,0:T(8,128)(2,1)} %bitcast.6), channel_id=1, source_target_pairs={{16,0},{17,1},{18,2},{19,3},{20,4},{21,5},{22,6},{23,7},{24,8},{25... | collective-permute-start | bytes 49160 | tf_op jit(solution)/shard_map/ppermute | solution.py:68
  6.5 0.0 copy-done.1
  6.5 0.0 copy-start.2
  6.5 0.7 %copy-done.2 = bf16[128,64]{0,1:T(8,128)(2,1)S(1)} copy-done((bf16[128,64]{0,1:T(8,128)(2,1)S(1)}, bf16[128,64]{0,1:T(8,128)(2,1)}, u32[]{:S(2)}) %copy-start.2) | copy-done | bytes 16408
  7.2 1.3 %collective-permute-start.1 = (bf16[64,128]{1,0:T(8,128)(2,1)S(1)}, bf16[64,128]{1,0:T(8,128)(2,1)S(1)}, u32[]{:S(2)}, u32[]{:S(2)}) collective-permute-start(bf16[64,128]{1,0:T(8,128)(2,1)S(1)} %bitcast.7), channel_id=1, source_target_pairs={{0,16},{1,17},{2,18},{3,19},{4,20},{5,21},{6,22},{7,23},{8,24},{9,... | collective-permute-start | bytes 49160 | tf_op jit(solution)/shard_map/ppermute | solution.py:76
  8.5 12.6 %conditional.3 = (bf16[8,16,256]{2,1,0:T(8,128)(2,1)S(1)}) conditional(s32[]{:T(128)} %convert_element_type.4, bf16[16,256]{1,0:T(8,128)(2,1)S(1)} %bitcast.5, bf16[8,16,256]{2,1,0:T(8,128)(2,1)S(1)} %get-tuple-element.18), branch_computations={%region_2.0_spmd, %region_3.0_spmd} | conditional | bytes 204808 | solution.py:77
  8.6 12.6 %all_to_all.14 = bf16[8,16,256]{2,1,0:T(8,128)(2,1)S(1)} all-to-all(bf16[8,16,256]{2,1,0:T(8,128)(2,1)S(1)} %broadcast_in_dim.9), channel_id=1, replica_groups={{320,384,448,256,192,128,64,0},{321,385,449,257,193,129,65,1},{322,386,..., dimensions={0} | all-to-all | bytes 131072 | tf_op jit(solution)/shard_map/cond/branch_0_fun/all_to_all | solution.py:18
  21.1 0.0 copy-start
  21.1 0.9 %broadcast_in_dim.16 = bf16[16,2,64,128]{3,2,1,0:T(8,128)(2,1)} broadcast(bf16[64,128]{1,0:T(8,128)(2,1)S(1)} %bitcast.8), dimensions={2,3} | broadcast | bytes 540672 | tf_op jit(solution)/shard_map/broadcast_in_dim | solution.py:79
  22.0 0.0 collective-permute-done
  22.1 0.1 collective-permute-done.1
  22.1 0.8 %broadcast_dynamic-update-slice_fusion = bf16[16,2,64,128]{3,2,1,0:T(8,128)(2,1)} fusion(bf16[16,2,64,128]{3,2,1,0:T(8,128)(2,1)} %broadcast_in_dim.16, s32[]{:T(128)S(6)} %select_n.15, bf16[64,128]{1,0:T(8,128)(2,1)S(1)} %broadcast_select_fusion), kind=kLoop, calls=%fused_computation | loop fusion | bytes 278532 | tf_op jit(solution)/shard_map/dynamic_update_slice | solution.py:83
  22.9 9.1 %all-to-all-start.2 = ((bf16[16,2,64,128]{3,2,1,0:T(8,128)(2,1)}), bf16[16,2,64,128]{3,2,1,0:T(8,128)(2,1)S(1)}, u32[]{:S(2)}, u32[]{:S(2)}) async-start(bf16[16,2,64,128]{3,2,1,0:T(8,128)(2,1)} %broadcast_dynamic-update-slice_fusion), calls=%async_computation.2 | async-start | bytes 1048576 | tf_op jit(solution)/shard_map/all_to_all | solution.py:84
  32.0 1.9 %all-gather = bf16[8,32,256]{2,1,0:T(8,128)(2,1)S(1)} all-gather(bf16[8,16,256]{2,1,0:T(8,128)(2,1)S(1)} %get-tuple-element.19), channel_id=2, replica_groups=mesh['z_lo'=8,'core'=2,'z_hi'=2,'y'=4,'x'=4] {'core'}, dimensions={1}, use_global_device_ids=true | all-gather | bytes 196608 | tf_op jit(solution)/shard_map/all_gather | solution.py:78
  33.8 3.3 %all-to-all-done.2.int_ref = bf16[16,2,64,128]{3,2,1,0:T(8,128)(2,1)S(1)} async-done(((bf16[16,2,64,128]{3,2,1,0:T(8,128)(2,1)}), bf16[16,2,64,128]{3,2,1,0:T(8,128)(2,1)S(1)}, u32[]{:S(2)}, u32[]{:S(2)}) %all-to-all-start.2) | async-done | bytes 524320 | tf_op jit(solution)/shard_map/all_to_all | solution.py:84
  37.1 0.0 copy-done
  37.1 1.3 %shard_map.37 = f32[256,1024]{1,0:T(8,128)} custom-call(bf16[8,2,16,256]{3,2,1,0:T(8,128)(2,1)S(1)} %bitcast.3, bf16[16,2,64,128]{3,2,1,0:T(8,128)(2,1)S(1)} %all-to-all-done.2.int_ref, f32[256,1024]{1,0:T(8,128)S(1)} %copy-done), custom_call_target="tpu_custom_call" | custom-call | flops 134217728 | bytes 2097152 | tf_op jit(solution)/shard_map/pallas_call | solution.py:49
  (4 shorter events, 0.0 us)
Async XLA Ops:
  0.0 6.5 %copy-start.1 = (bf16[256,16]{0,1:T(8,128)(2,1)S(1)}, bf16[256,16]{0,1:T(8,128)(2,1)}, u32[]{:S(2)}) copy-start(bf16[256,16]{0,1:T(8,128)(2,1)} %param.7) | copy-start | bytes 24580
  0.0 22.0 %collective-permute-start = (bf16[64,128]{1,0:T(8,128)(2,1)}, bf16[64,128]{1,0:T(8,128)(2,1)S(1)}, u32[]{:S(2)}, u32[]{:S(2)}) collective-permute-start(bf16[64,128]{1,0:T(8,128)(2,1)} %bitcast.6), channel_id=1, source_target_pairs={{16,0},{17,1},{18,2},{19,3},{20,4},{21,5},{22,6},{23,7},{24,8},{25... | collective-permute-start | bytes 49160 | tf_op jit(solution)/shard_map/ppermute | solution.py:68
  6.5 0.8 %copy-start.2 = (bf16[128,64]{0,1:T(8,128)(2,1)S(1)}, bf16[128,64]{0,1:T(8,128)(2,1)}, u32[]{:S(2)}) copy-start(bf16[128,64]{0,1:T(8,128)(2,1)} %param.8) | copy-start | bytes 49156
  7.2 14.9 %collective-permute-start.1 = (bf16[64,128]{1,0:T(8,128)(2,1)S(1)}, bf16[64,128]{1,0:T(8,128)(2,1)S(1)}, u32[]{:S(2)}, u32[]{:S(2)}) collective-permute-start(bf16[64,128]{1,0:T(8,128)(2,1)S(1)} %bitcast.7), channel_id=1, source_target_pairs={{0,16},{1,17},{2,18},{3,19},{4,20},{5,21},{6,22},{7,23},{8,24},{9,... | collective-permute-start | bytes 49160 | tf_op jit(solution)/shard_map/ppermute | solution.py:76
  21.1 16.0 %copy-start = (f32[256,1024]{1,0:T(8,128)S(1)}, f32[256,1024]{1,0:T(8,128)}, u32[]{:S(2)}) copy-start(f32[256,1024]{1,0:T(8,128)} %old_ref.1) | copy-start | bytes 3145732
  22.9 14.2 %all-to-all-start.2 = ((bf16[16,2,64,128]{3,2,1,0:T(8,128)(2,1)}), bf16[16,2,64,128]{3,2,1,0:T(8,128)(2,1)S(1)}, u32[]{:S(2)}, u32[]{:S(2)}) async-start(bf16[16,2,64,128]{3,2,1,0:T(8,128)(2,1)} %broadcast_dynamic-update-slice_fusion), calls=%async_computation.2 | async-start | bytes 1048576 | tf_op jit(solution)/shard_map/all_to_all | solution.py:84
